TPU v7x, 32 devices: a whole 2x2x4 slice. The times are simulated.
32 devices in a mesh: dp: 16 (over z, y, core), head: 2 (over x).
Axes of the slice: x: 2, y: 2, z: 4, core: 2. Of those that a mesh axis runs over, the one named last changes fastest.
Arguments:
- media_tokens: bfloat16 [256, 256, 1024], P('dp'), may hold values from -6 to 6
- latents: bfloat16 [256, 64, 1024], P('dp'), may hold values from -6 to 6
- cotangent: bfloat16 [256, 64, 1024], P('dp'), may hold values from -6 to 6
- image_counts: int32 [128], P('dp'), may hold values from 1 to 2, as said below
- media_gain: float32 [1024], replicated, may hold values from 0.1 to 1.9
- media_bias: float32 [1024], replicated, may hold values from -3 to 3
- latent_gain: float32 [1024], replicated, may hold values from 0.1 to 1.9
- latent_bias: float32 [1024], replicated, may hold values from -3 to 3
- ff_gain: float32 [1024], replicated, may hold values from 0.1 to 1.9
- ff_bias: float32 [1024], replicated, may hold values from -3 to 3
- w_query: bfloat16 [1024, 512], P('dp', 'head'), may hold values from -0.1875 to 0.1875
- w_keyval: bfloat16 [1024, 2, 512], P('dp', None, 'head'), may hold values from -0.1875 to 0.1875
- w_attn_out: bfloat16 [512, 1024], P('head', 'dp'), may hold values from -1 to 1
- w_up: bfloat16 [1024, 4096], P('dp', 'head'), may hold values from -0.1875 to 0.1875
- w_down: bfloat16 [4096, 1024], P('head', 'dp'), may hold values from -0.09375 to 0.09375
Outputs:
- latents_out: float32 [256, 64, 1024], P('dp', 'head')
- media_grad: float32 [256, 256, 1024], P('dp', 'head')
- latent_grad: float32 [256, 64, 1024], P('dp', 'head')
- grad_query: float32 [1024, 512], P('dp', 'head')
- grad_keyval: float32 [1024, 2, 512], P('dp', None, 'head')
- grad_attn_out: float32 [512, 1024], P('head', 'dp')
- grad_up: float32 [1024, 4096], P('dp', 'head')
- grad_down: float32 [4096, 1024], P('head', 'dp')
- norm_grads: float32 [6, 1024], replicated
Inputs may be any that keep to these rules, and one draw needn't show every extreme that they name: `image_counts`: samples are stored in order, 8 to each index of dp. The images of a dp index's samples fill its 16 slots from slot 0 on, sample after sample; the other slots of that index are empty. In every draw some sample has 2 images and some dp index has all its slots filled.
All inputs are finite; a program needn't handle non-finite values.
Results may differ from a plain program's by a relative error of at most 0.019.
Values may be sent and summed in bfloat16 or wider, within the bound.
No kernel may reach another device: no remote copies, remote signals or barrier semaphores. Data moves between devices by JAX's collectives and lax.ppermute only.
A program may use at most 192 MiB of HBM per device.

v0:
```python
import math
import jax
import jax.numpy as jnp
from jax import lax
from jax.sharding import PartitionSpec as P

HD = 64


def layer_norm(values, gain, bias):
    centre = values - jnp.mean(values, axis=-1, keepdims=True)
    spread = jnp.mean(centre * centre, axis=-1, keepdims=True)
    return centre * lax.rsqrt(spread + 1e-05) * gain + bias


def norm_back(values, gain, bias, grad):
    result, pull = jax.vjp(layer_norm, values, gain, bias)
    return pull(grad)


def gelu_exact(values):
    return jax.nn.gelu(values, approximate=False)


def row_share(values, count):
    start = lax.axis_index("head") * count
    return lax.dynamic_slice_in_dim(values, start, count, 1)


def local(
    media_tokens,
    latents,
    cotangent,
    image_counts,
    media_gain,
    media_bias,
    latent_gain,
    latent_bias,
    ff_gain,
    ff_bias,
    w_query,
    w_keyval,
    w_attn_out,
    w_up,
    w_down,
):
    images, patches = (media_tokens.shape[0], media_tokens.shape[1])
    lat_rows = latents.shape[1]
    head_count = w_query.shape[1] // HD
    head_groups = lax.axis_size("head")
    patch_share = patches // head_groups
    lat_share = lat_rows // head_groups
    score_scale = 1.0 / math.sqrt(HD)
    live_mask = (jnp.arange(images, dtype=jnp.int32) < jnp.sum(image_counts)).astype(jnp.float32)[
        :, None, None
    ]
    query_all, keyval_all, up_all = (
        lax.all_gather(w_query, "dp", axis=0, tiled=True),
        lax.all_gather(w_keyval, "dp", axis=0, tiled=True),
        lax.all_gather(w_up, "dp", axis=0, tiled=True),
    )
    attn_all, down_all = (
        lax.all_gather(w_attn_out, "dp", axis=1, tiled=True),
        lax.all_gather(w_down, "dp", axis=1, tiled=True),
    )
    media_full = media_tokens.astype(jnp.float32)
    latent_full = latents.astype(jnp.float32)
    normed_media = layer_norm(media_full, media_gain, media_bias).astype(jnp.bfloat16)
    normed_lat = layer_norm(latent_full, latent_gain, latent_bias).astype(jnp.bfloat16)
    sources = jnp.concatenate([normed_media, normed_lat], axis=1)
    src_rows = sources.shape[1]
    query_act = jnp.einsum(
        "ild,dc->ilc", normed_lat, query_all, preferred_element_type=jnp.float32
    ).astype(jnp.bfloat16)
    keyval = jnp.einsum(
        "ird,dkc->ikrc", sources, keyval_all, preferred_element_type=jnp.float32
    ).astype(jnp.bfloat16)
    query_blocks = query_act.reshape(images, lat_rows, head_count, HD)
    key_blocks = keyval[:, 0].reshape(images, src_rows, head_count, HD)
    value_blocks = keyval[:, 1].reshape(images, src_rows, head_count, HD)
    scores = (
        jnp.einsum("ilhe,irhe->ihlr", query_blocks, key_blocks, preferred_element_type=jnp.float32)
        * score_scale
    )
    row_top = jnp.max(scores, axis=-1, keepdims=True)
    exp_terms = jnp.exp(scores - row_top)
    row_total = jnp.sum(exp_terms, axis=-1, keepdims=True)
    probs_low = (exp_terms / row_total).astype(jnp.bfloat16)
    log_total = row_top + jnp.log(row_total)
    mixed_heads = (
        jnp.einsum("ihlr,irhe->ilhe", probs_low, value_blocks, preferred_element_type=jnp.float32)
        .astype(jnp.bfloat16)
        .reshape(images, lat_rows, head_count * HD)
    )
    attn_part = jnp.einsum("ilc,cd->ild", mixed_heads, attn_all, preferred_element_type=jnp.float32)
    middle = latent_full + lax.psum(attn_part.astype(jnp.bfloat16), "head").astype(jnp.float32)
    normed_mid = layer_norm(middle, ff_gain, ff_bias).astype(jnp.bfloat16)
    up_act = jnp.einsum("ild,df->ilf", normed_mid, up_all, preferred_element_type=jnp.float32)
    hidden, gelu_pull = jax.vjp(gelu_exact, up_act)
    hidden_low = hidden.astype(jnp.bfloat16)
    ff_part = jnp.einsum("ilf,fd->ild", hidden_low, down_all, preferred_element_type=jnp.float32)
    final_lat = middle + lax.psum(ff_part.astype(jnp.bfloat16), "head").astype(jnp.float32)
    latent_rows_share = row_share(latent_full, lat_share)
    latents_out = jnp.where(live_mask > 0, row_share(final_lat, lat_share), latent_rows_share)
    grad_final = cotangent.astype(jnp.float32) * live_mask
    final_low = grad_final.astype(jnp.bfloat16)
    grad_down = jnp.einsum("ilf,ild->fd", hidden_low, final_low, preferred_element_type=jnp.float32)
    grad_hidden = jnp.einsum("ild,fd->ilf", final_low, down_all, preferred_element_type=jnp.float32)
    up_low = gelu_pull(grad_hidden)[0].astype(jnp.bfloat16)
    grad_up = jnp.einsum("ild,ilf->df", normed_mid, up_low, preferred_element_type=jnp.float32)
    mid_part = jnp.einsum("ilf,df->ild", up_low, up_all, preferred_element_type=jnp.float32)
    grad_normed_mid = lax.psum(mid_part.astype(jnp.bfloat16), "head").astype(jnp.float32)
    mid_back, ff_gain_grad, ff_bias_grad = norm_back(middle, ff_gain, ff_bias, grad_normed_mid)
    grad_mid = grad_final + mid_back
    mid_low = grad_mid.astype(jnp.bfloat16)
    grad_attn = jnp.einsum("ilc,ild->cd", mixed_heads, mid_low, preferred_element_type=jnp.float32)
    grad_mixed = (
        jnp.einsum("ild,cd->ilc", mid_low, attn_all, preferred_element_type=jnp.float32)
        .astype(jnp.bfloat16)
        .reshape(images, lat_rows, head_count, HD)
    )
    scores_again = (
        jnp.einsum("ilhe,irhe->ihlr", query_blocks, key_blocks, preferred_element_type=jnp.float32)
        * score_scale
    )
    attn_probs = jnp.exp(scores_again - log_total)
    grad_values = jnp.einsum(
        "ihlr,ilhe->irhe", probs_low, grad_mixed, preferred_element_type=jnp.float32
    ).astype(jnp.bfloat16)
    grad_probs = jnp.einsum(
        "ilhe,irhe->ihlr", grad_mixed, value_blocks, preferred_element_type=jnp.float32
    )
    grad_scores = (
        attn_probs * (grad_probs - jnp.sum(attn_probs * grad_probs, axis=-1, keepdims=True))
    ).astype(jnp.bfloat16)
    grad_query_act = (
        (
            jnp.einsum(
                "ihlr,irhe->ilhe", grad_scores, key_blocks, preferred_element_type=jnp.float32
            )
            * score_scale
        )
        .astype(jnp.bfloat16)
        .reshape(images, lat_rows, head_count * HD)
    )
    grad_keys = (
        jnp.einsum("ihlr,ilhe->irhe", grad_scores, query_blocks, preferred_element_type=jnp.float32)
        * score_scale
    ).astype(jnp.bfloat16)
    grad_keyval_act = jnp.stack(
        [
            grad_keys.reshape(images, src_rows, head_count * HD),
            grad_values.reshape(images, src_rows, head_count * HD),
        ],
        axis=1,
    )
    grad_query = jnp.einsum(
        "ild,ilc->dc", normed_lat, grad_query_act, preferred_element_type=jnp.float32
    )
    grad_keyval = jnp.einsum(
        "ird,ikrc->dkc", sources, grad_keyval_act, preferred_element_type=jnp.float32
    )
    lat_part = jnp.einsum(
        "ikrc,dkc->ird",
        grad_keyval_act[:, :, patches:],
        keyval_all,
        preferred_element_type=jnp.float32,
    )
    lat_part = lat_part + jnp.einsum(
        "ilc,dc->ild", grad_query_act, query_all, preferred_element_type=jnp.float32
    )
    media_part = jnp.einsum(
        "ikrc,dkc->ird",
        grad_keyval_act[:, :, :patches],
        keyval_all,
        preferred_element_type=jnp.float32,
    )
    grad_normed_media, grad_normed_lat = (
        lax.psum_scatter(
            media_part.astype(jnp.bfloat16), "head", scatter_dimension=1, tiled=True
        ).astype(jnp.float32),
        lax.psum_scatter(
            lat_part.astype(jnp.bfloat16), "head", scatter_dimension=1, tiled=True
        ).astype(jnp.float32),
    )
    media_share = row_share(media_full, patch_share)
    media_grad, media_gain_grad, media_bias_grad = norm_back(
        media_share, media_gain, media_bias, grad_normed_media
    )
    lat_back, lat_gain_grad, lat_bias_grad = norm_back(
        latent_rows_share, latent_gain, latent_bias, grad_normed_lat
    )
    cot_share = row_share(cotangent.astype(jnp.float32), lat_share)
    latent_grad = jnp.where(live_mask > 0, row_share(grad_mid, lat_share) + lat_back, cot_share)
    gain_terms = jnp.stack(
        [
            media_gain_grad,
            media_bias_grad,
            lat_gain_grad,
            lat_bias_grad,
            ff_gain_grad / head_groups,
            ff_bias_grad / head_groups,
        ]
    )
    norm_grads = lax.psum(gain_terms, ("dp", "head"))
    grad_query, grad_keyval, grad_up = (
        lax.psum_scatter(
            grad_query.astype(jnp.bfloat16), "dp", scatter_dimension=0, tiled=True
        ).astype(jnp.float32),
        lax.psum_scatter(
            grad_keyval.astype(jnp.bfloat16), "dp", scatter_dimension=0, tiled=True
        ).astype(jnp.float32),
        lax.psum_scatter(
            grad_up.astype(jnp.bfloat16), "dp", scatter_dimension=0, tiled=True
        ).astype(jnp.float32),
    )
    grad_attn, grad_down = (
        lax.psum_scatter(
            grad_attn.astype(jnp.bfloat16), "dp", scatter_dimension=1, tiled=True
        ).astype(jnp.float32),
        lax.psum_scatter(
            grad_down.astype(jnp.bfloat16), "dp", scatter_dimension=1, tiled=True
        ).astype(jnp.float32),
    )
    return (
        latents_out,
        media_grad,
        latent_grad,
        grad_query,
        grad_keyval,
        grad_attn,
        grad_up,
        grad_down,
        norm_grads,
    )


def solution(mesh):
    return jax.shard_map(
        local,
        mesh=mesh,
        in_specs=(
            P("dp", None, None),
            P("dp", None, None),
            P("dp", None, None),
            P("dp"),
            P(),
            P(),
            P(),
            P(),
            P(),
            P(),
            P("dp", "head"),
            P("dp", None, "head"),
            P("head", "dp"),
            P("dp", "head"),
            P("head", "dp"),
        ),
        out_specs=(
            P("dp", "head", None),
            P("dp", "head", None),
            P("dp", "head", None),
            P("dp", "head"),
            P("dp", None, "head"),
            P("head", "dp"),
            P("dp", "head"),
            P("head", "dp"),
            P(),
        ),
        check_vma=False,
    )
```

profile of v0, /device:TPU:0, one launch (start us, length us, event | category | flops | bytes accessed | tf_op | source)
XLA Modules:
  0.0 992.0 jit_solution(9586764897184007495)
XLA Ops:
  21.6 25.3 %all_gather.16 = bf16[1024,256]{1,0:T(8,128)(2,1)S(1)} all-gather(bf16[64,256]{1,0:T(8,128)(2,1)S(1)} %copy-done.29), channel_id=1, replica_groups=mesh['dp'=16,'head'=2] {'dp'}, dimensions={0}, use_global_device_ids=true | all-gather | bytes 557056 | tf_op jit(solution)/shard_map/all_gather | solution.py:58
  52.2 20.8 %all_gather.17 = bf16[256,1024]{0,1:T(8,128)(2,1)} all-gather(bf16[256,64]{0,1:T(8,128)(2,1)S(1)} %copy-done.30), channel_id=1, replica_groups=mesh['dp'=16,'head'=2] {'dp'}, dimensions={1}, use_global_device_ids=true | all-gather | bytes 557056 | tf_op jit(solution)/shard_map/all_gather | solution.py:63
  73.0 8.6 add_convert_fusion
  81.6 8.6 convert_bitcast_fusion
  119.9 59.0 %all-reduce.4.cloned.1.call-done = bf16[16,64,1024]{2,1,0:T(8,128)(2,1)} async-done(((bf16[16,64,1024]{2,1,0:T(8,128)(2,1)}), bf16[16,64,1024]{2,1,0:T(8,128)(2,1)}) %all-reduce.4.cloned.1.call-update) | async-done | bytes 2097168 | tf_op jit(solution)/shard_map/psum | solution.py:96
  182.2 49.7 %all-gather.6.cloned.1.call-done = bf16[1024,2048]{1,0:T(8,128)(2,1)} async-done(((bf16[64,2048]{1,0:T(8,128)(2,1)}), bf16[1024,2048]{1,0:T(8,128)(2,1)}) %all-gather.6.cloned.1.call-update) | async-done | bytes 4194320 | tf_op jit(solution)/shard_map/all_gather | solution.py:60
  231.9 9.4 fusion.28
  244.5 19.8 %multiply_convert_fusion = (bf16[16,64,2048]{2,1,0:T(8,128)(2,1)}, f32[16,64,2048]{2,1,0:T(8,128)}) fusion(f32[16,64,2048]{2,1,0:T(8,128)S(1)} %get-tuple-element.59, u16[64,2048]{1,0:T(8,128)(2,1)S(1)} %get-tuple-element.32, u16[64,2048]{1,0:T(8,128)(2,1)S(1)} %get-tuple-element.31), kind=kLoop, calls=%fused_computation.24 | loop fusion | flops 146800640 | bytes 21495808 | tf_op jit(solution)/shard_map/convert_element_type | solution.py:100
  264.3 18.9 %all-gather.8.cloned.1.call-done = bf16[2048,1024]{0,1:T(8,128)(2,1)} async-done(((bf16[2048,64]{0,1:T(8,128)(2,1)}), bf16[2048,1024]{0,1:T(8,128)(2,1)}) %all-gather.8.cloned.1.call-update) | async-done | bytes 4194320 | tf_op jit(solution)/shard_map/all_gather | solution.py:64
  283.2 12.8 %add_convert_fusion.1 = bf16[16,64,2048]{2,1,0:T(8,128)(2,1)S(1)} fusion(f32[16,64,2048]{2,1,0:T(8,128)} %get-tuple-element.46, f32[16,64,2048]{2,1,0:T(8,128)} %copy-done.11, bf16[2048,1024]{0,1:T(8,128)(2,1)} %all-gather.8.cloned.1.call-done, f32[16]{0:T(128)S(1)} %compare_convert_fusion, bf16[16,64,1024]{2,1,0:T(8,128)(2,1)} %param.17), kind=kOutput, calls=%fused_computation.23 | convolution fusion | flops 4327473152 | bytes 27263040 | tf_op jit(solution)/shard_map/ild,fd->ilf/dot_general | solution.py:108
  307.7 106.8 %all-reduce.6.cloned.1.call-done = (bf16[16,64,1024]{2,1,0:T(8,128)(2,1)}, bf16[16,64,1024]{2,1,0:T(8,128)(2,1)}) async-done(((bf16[16,64,1024]{2,1,0:T(8,128)(2,1)}, bf16[16,64,1024]{2,1,0:T(8,128)(2,1)}), (bf16[16,64,1024]{2,1,0:T(8,128)(2,1)}, bf16[16,64,1024]{2,1,0:T(8,128)(2,1)})) %all-reduce.6.cloned.1.call-update) | async-done | bytes 4194320 | tf_op jit(solution)/shard_map/psum | solution.py:112
  466.0 10.8 %bitcast_convert_fusion.3 = bf16[1024,2,256]{2,0,1:T(8,128)(2,1)} fusion(bf16[16,1,320,256]{3,2,1,0:T(8,128)(2,1)} %copy.50, bf16[16,1,320,256]{3,2,1,0:T(8,128)(2,1)} %copy.49, bf16[16,64,1024]{2,1,0:T(8,128)(2,1)} %copy-done.19, bf16[16,256,1024]{2,1,0:T(8,128)(2,1)} %add_convert_fusion), kind=kOutput, calls=%fused_computation.96 | convolution fusion | flops 5400690688 | bytes 16777216 | tf_op jit(solution)/shard_map/ird,ikrc->dkc/dot_general | solution.py:160
  476.9 9.7 bitcast_convert_fusion.2
  486.9 9.5 bitcast_convert_fusion.1
  502.3 10.5 %bitcast_convert_fusion = bf16[16,256,1024]{2,1,0:T(8,128)(2,1)} fusion(bf16[16,1,320,256]{3,2,1,0:T(8,128)(2,1)} %copy.49, bf16[16,1,320,256]{3,2,1,0:T(8,128)(2,1)} %copy.50, bf16[1024,2,256]{2,0,1:T(8,128)(2,1)} %all-gather.4.cloned.1.call-done), kind=kOutput, calls=%fused_computation | convolution fusion | flops 4301258752 | bytes 14680064 | tf_op jit(solution)/shard_map/ikrc,dkc->ird/dot_general | solution.py:172
  512.9 11.3 %convert_element_type.145 = f32[16,256,1024]{2,1,0:T(8,128)} convert(bf16[16,256,1024]{2,1,0:T(8,128)(2,1)} %param.15) | non-fusion elementwise | flops 4194304 | bytes 25165824 | tf_op jit(solution)/shard_map/convert_element_type | solution.py:66
  537.2 37.4 %reduce-scatter.12.cloned.1.call-done = bf16[64,256]{1,0:T(8,128)(2,1)} async-done(((bf16[1024,256]{1,0:T(8,128)(2,1)}), bf16[64,256]{1,0:T(8,128)(2,1)}) %reduce-scatter.12.cloned.1.call-update) | async-done | bytes 32784 | tf_op jit(solution)/shard_map/reduce_scatter | solution.py:207
  576.0 59.2 %reduce-scatter.14.cloned.1.call-done = bf16[64,2,256]{2,0,1:T(8,128)(2,1)} async-done(((bf16[1024,2,256]{2,0,1:T(8,128)(2,1)}), bf16[64,2,256]{2,0,1:T(8,128)(2,1)}) %reduce-scatter.14.cloned.1.call-update) | async-done | bytes 65552 | tf_op jit(solution)/shard_map/reduce_scatter | solution.py:210
  636.7 74.5 %reduce-scatter.18.cloned.1.call-done = bf16[64,2048]{1,0:T(8,128)(2,1)} async-done(((bf16[1024,2048]{1,0:T(8,128)(2,1)}), bf16[64,2048]{1,0:T(8,128)(2,1)}) %reduce-scatter.18.cloned.1.call-update) | async-done | bytes 262160 | tf_op jit(solution)/shard_map/reduce_scatter | solution.py:213
  713.0 73.5 %reduce-scatter.20.cloned.1.call-done = bf16[2048,64]{0,1:T(8,128)(2,1)} async-done(((bf16[2048,1024]{0,1:T(8,128)(2,1)}), bf16[2048,64]{0,1:T(8,128)(2,1)}) %reduce-scatter.20.cloned.1.call-update) | async-done | bytes 262160 | tf_op jit(solution)/shard_map/reduce_scatter | solution.py:221
  788.2 32.0 %reduce-scatter.10.cloned.1.call-done = bf16[16,32,1024]{2,1,0:T(8,128)(2,1)} async-done(((bf16[16,64,1024]{2,1,0:T(8,128)(2,1)}), bf16[16,32,1024]{2,1,0:T(8,128)(2,1)}) %reduce-scatter.10.cloned.1.call-update) | async-done | bytes 1048592 | tf_op jit(solution)/shard_map/reduce_scatter | solution.py:182
  831.9 90.3 %reduce-scatter.8.cloned.1.call-done = bf16[16,128,1024]{2,1,0:T(8,128)(2,1)} async-done(((bf16[16,256,1024]{2,1,0:T(8,128)(2,1)}), bf16[16,128,1024]{2,1,0:T(8,128)(2,1)}) %reduce-scatter.8.cloned.1.call-update) | async-done | bytes 4194320 | tf_op jit(solution)/shard_map/reduce_scatter | solution.py:179
  936.5 40.0 %psum.31 = f32[6,1024]{1,0:T(8,128)} all-reduce(f32[6,1024]{1,0:T(8,128)S(1)} %stack.25), channel_id=1, replica_groups=mesh['dp'=16,'head'=2] {'dp','head'}, use_global_device_ids=true, to_apply=%region_36.37 | all-reduce | flops 6144 | bytes 49152 | tf_op jit(solution)/shard_map/psum | solution.py:205
  976.6 8.1 broadcast_add_fusion
  (178 shorter events, 170.3 us)
Async XLA Ops:
  7.2 74.4 %all-gather.4.cloned.1.call-start = ((), (), s32[]{:S(2)}) async-start(), calls=%async_computation.7 | async-start | bytes 1114112 | tf_op jit(solution)/shard_map/all_gather | solution.py:59
  8.7 170.1 %all-reduce.4.cloned.1.call-start = ((), (), s32[]{:S(2)}) async-start(), calls=%async_computation.8 | async-start | bytes 4194304 | tf_op jit(solution)/shard_map/psum | solution.py:96
  18.8 28.1 %copy-start = (bf16[16,64,1024]{2,1,0:T(8,128)(2,1)S(1)}, bf16[16,64,1024]{2,1,0:T(8,128)(2,1)}, u32[]{:S(2)}) copy-start(bf16[16,64,1024]{2,1,0:T(8,128)(2,1)} %param.16) | copy-start | bytes 6291460
  18.8 28.1 %copy-start.24 = (f32[1024]{0:T(1024)S(1)}, f32[1024]{0:T(1024)}, u32[]{:S(2)}) copy-start(f32[1024]{0:T(1024)} %param.21) | copy-start | bytes 12292
  18.8 28.1 %copy-start.31 = (f32[1024]{0:T(1024)S(1)}, f32[1024]{0:T(1024)}, u32[]{:S(2)}) copy-start(f32[1024]{0:T(1024)} %param.22) | copy-start | bytes 12292
  46.9 26.0 %copy-start.26 = (f32[1024]{0:T(1024)S(1)}, f32[1024]{0:T(1024)}, u32[]{:S(2)}) copy-start(f32[1024]{0:T(1024)} %param.19) | copy-start | bytes 12292
  47.0 26.0 %copy-start.32 = (f32[1024]{0:T(1024)S(1)}, f32[1024]{0:T(1024)}, u32[]{:S(2)}) copy-start(f32[1024]{0:T(1024)} %param.20) | copy-start | bytes 12292
  117.1 114.8 %all-gather.6.cloned.1.call-start = ((), (), s32[]{:S(2)}) async-start(), calls=%async_computation.9 | async-start | bytes 4456448 | tf_op jit(solution)/shard_map/all_gather | solution.py:60
  117.8 165.4 %all-gather.8.cloned.1.call-start = ((), (), s32[]{:S(2)}) async-start(), calls=%async_computation.10 | async-start | bytes 4456448 | tf_op jit(solution)/shard_map/all_gather | solution.py:64
  118.4 296.1 %all-reduce.6.cloned.1.call-start = ((), (), s32[]{:S(2)}) async-start(), calls=%async_computation.18 | async-start | bytes 8388608 | tf_op jit(solution)/shard_map/psum | solution.py:112
  119.9 112.0 %copy-start.28 = (f32[1024]{0:T(1024)S(1)}, f32[1024]{0:T(1024)}, u32[]{:S(2)}) copy-start(f32[1024]{0:T(1024)} %param.23) | copy-start | bytes 12292
  119.9 112.0 %copy-start.35 = (f32[1024]{0:T(1024)S(1)}, f32[1024]{0:T(1024)}, u32[]{:S(2)}) copy-start(f32[1024]{0:T(1024)} %param.24) | copy-start | bytes 12292
  283.2 12.8 %copy-start.33 = (bf16[1024,2048]{1,0:T(8,128)(2,1)S(1)}, bf16[1024,2048]{1,0:T(8,128)(2,1)}, u32[]{:S(2)}) copy-start(bf16[1024,2048]{1,0:T(8,128)(2,1)} %all-gather.6.cloned.1.call-done) | copy-start | bytes 12582916
  307.7 228.0 %reduce-scatter.16.cloned.1.call-start = ((), (), s32[]{:S(2)}) async-start(), calls=%async_computation.15 | async-start | bytes 557056 | tf_op jit(solution)/shard_map/reduce_scatter | solution.py:218
  459.3 115.3 %reduce-scatter.12.cloned.1.call-start = ((), (), s32[]{:S(2)}) async-start(), calls=%async_computation.13 | async-start | bytes 557056 | tf_op jit(solution)/shard_map/reduce_scatter | solution.py:207
  465.9 169.2 %reduce-scatter.14.cloned.1.call-start = ((), (), s32[]{:S(2)}) async-start(), calls=%async_computation.14 | async-start | bytes 1114112 | tf_op jit(solution)/shard_map/reduce_scatter | solution.py:210
  476.8 234.4 %reduce-scatter.18.cloned.1.call-start = ((), (), s32[]{:S(2)}) async-start(), calls=%async_computation.16 | async-start | bytes 4456448 | tf_op jit(solution)/shard_map/reduce_scatter | solution.py:213
  486.6 299.9 %reduce-scatter.20.cloned.1.call-start = ((), (), s32[]{:S(2)}) async-start(), calls=%async_computation.17 | async-start | bytes 4456448 | tf_op jit(solution)/shard_map/reduce_scatter | solution.py:221
  496.4 323.8 %reduce-scatter.10.cloned.1.call-start = ((), (), s32[]{:S(2)}) async-start(), calls=%async_computation.12 | async-start | bytes 3145728 | tf_op jit(solution)/shard_map/reduce_scatter | solution.py:182
  502.0 420.2 %reduce-scatter.8.cloned.1.call-start = ((), (), s32[]{:S(2)}) async-start(), calls=%async_computation.11 | async-start | bytes 12582912 | tf_op jit(solution)/shard_map/reduce_scatter | solution.py:179
  531.0 289.2 %copy-start.25 = (f32[1024]{0:T(1024)S(1)}, f32[1024]{0:T(1024)}, u32[]{:S(2)}) copy-start(f32[1024]{0:T(1024)} %param.21) | copy-start | bytes 12292
  535.6 290.7 %copy-start.23 = (bf16[16,64,1024]{2,1,0:T(8,128)(2,1)S(1)}, bf16[16,64,1024]{2,1,0:T(8,128)(2,1)}, u32[]{:S(2)}) copy-start(bf16[16,64,1024]{2,1,0:T(8,128)(2,1)} %get-tuple-element.44) | copy-start | bytes 6291460
  826.3 95.9 %copy-start.27 = (f32[1024]{0:T(1024)S(1)}, f32[1024]{0:T(1024)}, u32[]{:S(2)}) copy-start(f32[1024]{0:T(1024)} %param.19) | copy-start | bytes 12292
  922.2 7.6 copy-start.5
  (28 other events, 110.9 us)
Sparse Core Ops, SparseCore 0:
  10.8 41.0 all-gather.3
  117.2 61.6 all-reduce.3
  181.3 50.5 all-gather.5
  234.1 49.0 all-gather.7
  307.8 106.6 all-reduce.5
  459.4 55.7 reduce-scatter.15
  519.8 54.7 reduce-scatter.11
  578.8 56.3 reduce-scatter.13
  639.5 71.7 reduce-scatter.17
  714.9 71.4 reduce-scatter.19
  789.4 30.7 reduce-scatter.9
  822.9 99.2 reduce-scatter.7
where the time goes:
time: 997 us; the launch traced here: 992 us
  waiting for transfers between devices  603 us (60%)
  other arithmetic  125 us (13%)
  matrix products  124 us (12%)
  blocking collectives  86.1 us (9%)
  local copies, waits for them, and re-layouts  37.1 us (4%)
  between operations  15.3 us (2%)
    psum x1, waiting for transfers between devices, local(): lax.psum(mid_part.astype(jnp.bfloat16), 'head').astype(jnp.float32)  107 us
    reduce_scatter x1, waiting for transfers between devices, local(): lax.psum_scatter(media_part.astype(jnp.bfloat16), 'head', scatter_dimensi...  90.3 us
    reduce_scatter x1, waiting for transfers between devices, local(): lax.psum_scatter(grad_up.astype(jnp.bfloat16), 'dp', scatter_dimension=0,...  74.5 us
    reduce_scatter x1, waiting for transfers between devices, local(): lax.psum_scatter(grad_down.astype(jnp.bfloat16), 'dp', scatter_dimension=...  73.5 us
    reduce_scatter x1, waiting for transfers between devices, local(): lax.psum_scatter(grad_keyval.astype(jnp.bfloat16), 'dp', scatter_dimensio...  59.2 us
    psum x1, waiting for transfers between devices, local(): lax.psum(attn_part.astype(jnp.bfloat16), 'head').astype(jnp.float32)  59 us
    all_gather x1, waiting for transfers between devices, local(): lax.all_gather(w_up, 'dp', axis=0, tiled=True)  49.7 us
    psum x1, blocking collectives, local(): norm_grads = lax.psum(gain_terms, ('dp', 'head'))  40 us
  transfers between devices with their start and end apart: 12, of which 10 were waited for; matrix products, arithmetic and copies ran while one was open for 15% of the time, Pallas kernels for 0%

commit v1 on v0

--- a/solution.py
+++ b/solution.py
@@ -1,10 +1,21 @@
+import functools
 import math
 import jax
 import jax.numpy as jnp
 from jax import lax
 from jax.sharding import PartitionSpec as P
+from jax.lax import psum
 
 HD = 64
+
+
+def _note_edges(local_x, which_axis, shard_axis):
+    for rr in (which_axis, shard_axis):
+        local_x = psum(local_x, rr)
+    return local_x
+
+
+supply_masks_in = functools.partial(_note_edges, which_axis="head", shard_axis="dp")
 
 
 def layer_norm(values, gain, bias):
@@ -202,7 +213,7 @@
             ff_bias_grad / head_groups,
         ]
     )
-    norm_grads = lax.psum(gain_terms, ("dp", "head"))
+    norm_grads = supply_masks_in(gain_terms)
     grad_query, grad_keyval, grad_up = (
         lax.psum_scatter(
             grad_query.astype(jnp.bfloat16), "dp", scatter_dimension=0, tiled=True

time: 997 us -> 1020 us (1.023)
  blocking collectives: 86.1 us -> 113 us
    psum x1 -> x2, blocking collectives: 40 us -> 67.2 us  [_note_edges(): local_x = psum(local_x, rr)]
where the time goes in v1:
time: 1020 us
  waiting for transfers between devices  603 us (59%)
  other arithmetic  125 us (12%)
  matrix products  124 us (12%)
  blocking collectives  113 us (11%)
  local copies, waits for them, and re-layouts  37.1 us (4%)
  between operations  15.3 us (2%)
    psum x1, waiting for transfers between devices, local(): lax.psum(mid_part.astype(jnp.bfloat16), 'head').astype(jnp.float32)  107 us
    reduce_scatter x1, waiting for transfers between devices, local(): lax.psum_scatter(media_part.astype(jnp.bfloat16), 'head', scatter_dimensi...  90.3 us
    reduce_scatter x1, waiting for transfers between devices, local(): lax.psum_scatter(grad_up.astype(jnp.bfloat16), 'dp', scatter_dimension=0,...  74.5 us
    reduce_scatter x1, waiting for transfers between devices, local(): lax.psum_scatter(grad_down.astype(jnp.bfloat16), 'dp', scatter_dimension=...  73.5 us
    psum x2, blocking collectives, _note_edges(): local_x = psum(local_x, rr)  67.2 us
    reduce_scatter x1, waiting for transfers between devices, local(): lax.psum_scatter(grad_keyval.astype(jnp.bfloat16), 'dp', scatter_dimensio...  59.2 us
    psum x1, waiting for transfers between devices, local(): lax.psum(attn_part.astype(jnp.bfloat16), 'head').astype(jnp.float32)  59 us
    all_gather x1, waiting for transfers between devices, local(): lax.all_gather(w_up, 'dp', axis=0, tiled=True)  49.7 us
  transfers between devices with their start and end apart: 12, of which 10 were waited for; matrix products, arithmetic and copies ran while one was open for 15% of the time, Pallas kernels for 0%

profile of v1, /device:TPU:0, one launch (start us, length us, event | category | flops | bytes accessed | tf_op | source)
XLA Modules:
  0.0 1019.2 jit_solution(5909180293752316863)
XLA Ops:
  21.6 25.3 %all_gather.16 = bf16[1024,256]{1,0:T(8,128)(2,1)S(1)} all-gather(bf16[64,256]{1,0:T(8,128)(2,1)S(1)} %copy-done.29), channel_id=1, replica_groups=mesh['dp'=16,'head'=2] {'dp'}, dimensions={0}, use_global_device_ids=true | all-gather | bytes 557056 | tf_op jit(solution)/shard_map/all_gather | solution.py:69
  52.2 20.8 %all_gather.17 = bf16[256,1024]{0,1:T(8,128)(2,1)} all-gather(bf16[256,64]{0,1:T(8,128)(2,1)S(1)} %copy-done.30), channel_id=1, replica_groups=mesh['dp'=16,'head'=2] {'dp'}, dimensions={1}, use_global_device_ids=true | all-gather | bytes 557056 | tf_op jit(solution)/shard_map/all_gather | solution.py:74
  73.0 8.6 add_convert_fusion
  81.6 8.6 convert_bitcast_fusion
  119.9 59.0 %all-reduce.4.cloned.1.call-done = bf16[16,64,1024]{2,1,0:T(8,128)(2,1)} async-done(((bf16[16,64,1024]{2,1,0:T(8,128)(2,1)}), bf16[16,64,1024]{2,1,0:T(8,128)(2,1)}) %all-reduce.4.cloned.1.call-update) | async-done | bytes 2097168 | tf_op jit(solution)/shard_map/psum | solution.py:107
  182.2 49.7 %all-gather.6.cloned.1.call-done = bf16[1024,2048]{1,0:T(8,128)(2,1)} async-done(((bf16[64,2048]{1,0:T(8,128)(2,1)}), bf16[1024,2048]{1,0:T(8,128)(2,1)}) %all-gather.6.cloned.1.call-update) | async-done | bytes 4194320 | tf_op jit(solution)/shard_map/all_gather | solution.py:71
  231.9 9.4 fusion.28
  244.5 19.8 %multiply_convert_fusion = (bf16[16,64,2048]{2,1,0:T(8,128)(2,1)}, f32[16,64,2048]{2,1,0:T(8,128)}) fusion(f32[16,64,2048]{2,1,0:T(8,128)S(1)} %get-tuple-element.59, u16[64,2048]{1,0:T(8,128)(2,1)S(1)} %get-tuple-element.32, u16[64,2048]{1,0:T(8,128)(2,1)S(1)} %get-tuple-element.31), kind=kLoop, calls=%fused_computation.24 | loop fusion | flops 146800640 | bytes 21495808 | tf_op jit(solution)/shard_map/convert_element_type | solution.py:111
  264.3 18.9 %all-gather.8.cloned.1.call-done = bf16[2048,1024]{0,1:T(8,128)(2,1)} async-done(((bf16[2048,64]{0,1:T(8,128)(2,1)}), bf16[2048,1024]{0,1:T(8,128)(2,1)}) %all-gather.8.cloned.1.call-update) | async-done | bytes 4194320 | tf_op jit(solution)/shard_map/all_gather | solution.py:75
  283.2 12.8 %add_convert_fusion.1 = bf16[16,64,2048]{2,1,0:T(8,128)(2,1)S(1)} fusion(f32[16,64,2048]{2,1,0:T(8,128)} %get-tuple-element.46, f32[16,64,2048]{2,1,0:T(8,128)} %copy-done.11, bf16[2048,1024]{0,1:T(8,128)(2,1)} %all-gather.8.cloned.1.call-done, f32[16]{0:T(128)S(1)} %compare_convert_fusion, bf16[16,64,1024]{2,1,0:T(8,128)(2,1)} %param.17), kind=kOutput, calls=%fused_computation.23 | convolution fusion | flops 4327473152 | bytes 27263040 | tf_op jit(solution)/shard_map/ild,fd->ilf/dot_general | solution.py:119
  307.7 106.8 %all-reduce.6.cloned.1.call-done = (bf16[16,64,1024]{2,1,0:T(8,128)(2,1)}, bf16[16,64,1024]{2,1,0:T(8,128)(2,1)}) async-done(((bf16[16,64,1024]{2,1,0:T(8,128)(2,1)}, bf16[16,64,1024]{2,1,0:T(8,128)(2,1)}), (bf16[16,64,1024]{2,1,0:T(8,128)(2,1)}, bf16[16,64,1024]{2,1,0:T(8,128)(2,1)})) %all-reduce.6.cloned.1.call-update) | async-done | bytes 4194320 | tf_op jit(solution)/shard_map/psum | solution.py:123
  466.0 10.8 %bitcast_convert_fusion.3 = bf16[1024,2,256]{2,0,1:T(8,128)(2,1)} fusion(bf16[16,1,320,256]{3,2,1,0:T(8,128)(2,1)} %copy.50, bf16[16,1,320,256]{3,2,1,0:T(8,128)(2,1)} %copy.49, bf16[16,64,1024]{2,1,0:T(8,128)(2,1)} %copy-done.19, bf16[16,256,1024]{2,1,0:T(8,128)(2,1)} %add_convert_fusion), kind=kOutput, calls=%fused_computation.96 | convolution fusion | flops 5400690688 | bytes 16777216 | tf_op jit(solution)/shard_map/ird,ikrc->dkc/dot_general | solution.py:171
  476.9 9.7 bitcast_convert_fusion.2
  486.9 9.5 bitcast_convert_fusion.1
  502.3 10.5 %bitcast_convert_fusion = bf16[16,256,1024]{2,1,0:T(8,128)(2,1)} fusion(bf16[16,1,320,256]{3,2,1,0:T(8,128)(2,1)} %copy.49, bf16[16,1,320,256]{3,2,1,0:T(8,128)(2,1)} %copy.50, bf16[1024,2,256]{2,0,1:T(8,128)(2,1)} %all-gather.4.cloned.1.call-done), kind=kOutput, calls=%fused_computation | convolution fusion | flops 4301258752 | bytes 14680064 | tf_op jit(solution)/shard_map/ikrc,dkc->ird/dot_general | solution.py:183
  512.9 11.3 %convert_element_type.145 = f32[16,256,1024]{2,1,0:T(8,128)} convert(bf16[16,256,1024]{2,1,0:T(8,128)(2,1)} %param.15) | non-fusion elementwise | flops 4194304 | bytes 25165824 | tf_op jit(solution)/shard_map/convert_element_type | solution.py:77
  537.2 37.4 %reduce-scatter.12.cloned.1.call-done = bf16[64,256]{1,0:T(8,128)(2,1)} async-done(((bf16[1024,256]{1,0:T(8,128)(2,1)}), bf16[64,256]{1,0:T(8,128)(2,1)}) %reduce-scatter.12.cloned.1.call-update) | async-done | bytes 32784 | tf_op jit(solution)/shard_map/reduce_scatter | solution.py:218
  576.0 59.2 %reduce-scatter.14.cloned.1.call-done = bf16[64,2,256]{2,0,1:T(8,128)(2,1)} async-done(((bf16[1024,2,256]{2,0,1:T(8,128)(2,1)}), bf16[64,2,256]{2,0,1:T(8,128)(2,1)}) %reduce-scatter.14.cloned.1.call-update) | async-done | bytes 65552 | tf_op jit(solution)/shard_map/reduce_scatter | solution.py:221
  636.7 74.5 %reduce-scatter.18.cloned.1.call-done = bf16[64,2048]{1,0:T(8,128)(2,1)} async-done(((bf16[1024,2048]{1,0:T(8,128)(2,1)}), bf16[64,2048]{1,0:T(8,128)(2,1)}) %reduce-scatter.18.cloned.1.call-update) | async-done | bytes 262160 | tf_op jit(solution)/shard_map/reduce_scatter | solution.py:224
  713.0 73.5 %reduce-scatter.20.cloned.1.call-done = bf16[2048,64]{0,1:T(8,128)(2,1)} async-done(((bf16[2048,1024]{0,1:T(8,128)(2,1)}), bf16[2048,64]{0,1:T(8,128)(2,1)}) %reduce-scatter.20.cloned.1.call-update) | async-done | bytes 262160 | tf_op jit(solution)/shard_map/reduce_scatter | solution.py:232
  788.2 32.0 %reduce-scatter.10.cloned.1.call-done = bf16[16,32,1024]{2,1,0:T(8,128)(2,1)} async-done(((bf16[16,64,1024]{2,1,0:T(8,128)(2,1)}), bf16[16,32,1024]{2,1,0:T(8,128)(2,1)}) %reduce-scatter.10.cloned.1.call-update) | async-done | bytes 1048592 | tf_op jit(solution)/shard_map/reduce_scatter | solution.py:193
  831.9 90.3 %reduce-scatter.8.cloned.1.call-done = bf16[16,128,1024]{2,1,0:T(8,128)(2,1)} async-done(((bf16[16,256,1024]{2,1,0:T(8,128)(2,1)}), bf16[16,128,1024]{2,1,0:T(8,128)(2,1)}) %reduce-scatter.8.cloned.1.call-update) | async-done | bytes 4194320 | tf_op jit(solution)/shard_map/reduce_scatter | solution.py:190
  943.7 60.0 %psum.39 = f32[6,1024]{1,0:T(8,128)} all-reduce(f32[6,1024]{1,0:T(8,128)S(1)} %psum.38), channel_id=1, replica_groups=mesh['dp'=16,'head'=2] {'dp'}, use_global_device_ids=true, to_apply=%region_37.38 | all-reduce | flops 6144 | bytes 49152 | tf_op jit(solution)/shard_map/psum | solution.py:14
  1003.8 8.1 broadcast_add_fusion
  (179 shorter events, 177.5 us)
Async XLA Ops:
  7.2 74.4 %all-gather.4.cloned.1.call-start = ((), (), s32[]{:S(2)}) async-start(), calls=%async_computation.7 | async-start | bytes 1114112 | tf_op jit(solution)/shard_map/all_gather | solution.py:70
  8.7 170.1 %all-reduce.4.cloned.1.call-start = ((), (), s32[]{:S(2)}) async-start(), calls=%async_computation.8 | async-start | bytes 4194304 | tf_op jit(solution)/shard_map/psum | solution.py:107
  18.8 28.1 %copy-start = (bf16[16,64,1024]{2,1,0:T(8,128)(2,1)S(1)}, bf16[16,64,1024]{2,1,0:T(8,128)(2,1)}, u32[]{:S(2)}) copy-start(bf16[16,64,1024]{2,1,0:T(8,128)(2,1)} %param.16) | copy-start | bytes 6291460
  18.8 28.1 %copy-start.24 = (f32[1024]{0:T(1024)S(1)}, f32[1024]{0:T(1024)}, u32[]{:S(2)}) copy-start(f32[1024]{0:T(1024)} %param.21) | copy-start | bytes 12292
  18.8 28.1 %copy-start.31 = (f32[1024]{0:T(1024)S(1)}, f32[1024]{0:T(1024)}, u32[]{:S(2)}) copy-start(f32[1024]{0:T(1024)} %param.22) | copy-start | bytes 12292
  46.9 26.0 %copy-start.26 = (f32[1024]{0:T(1024)S(1)}, f32[1024]{0:T(1024)}, u32[]{:S(2)}) copy-start(f32[1024]{0:T(1024)} %param.19) | copy-start | bytes 12292
  47.0 26.0 %copy-start.32 = (f32[1024]{0:T(1024)S(1)}, f32[1024]{0:T(1024)}, u32[]{:S(2)}) copy-start(f32[1024]{0:T(1024)} %param.20) | copy-start | bytes 12292
  117.1 114.8 %all-gather.6.cloned.1.call-start = ((), (), s32[]{:S(2)}) async-start(), calls=%async_computation.9 | async-start | bytes 4456448 | tf_op jit(solution)/shard_map/all_gather | solution.py:71
  117.8 165.4 %all-gather.8.cloned.1.call-start = ((), (), s32[]{:S(2)}) async-start(), calls=%async_computation.10 | async-start | bytes 4456448 | tf_op jit(solution)/shard_map/all_gather | solution.py:75
  118.4 296.1 %all-reduce.6.cloned.1.call-start = ((), (), s32[]{:S(2)}) async-start(), calls=%async_computation.18 | async-start | bytes 8388608 | tf_op jit(solution)/shard_map/psum | solution.py:123
  119.9 112.0 %copy-start.28 = (f32[1024]{0:T(1024)S(1)}, f32[1024]{0:T(1024)}, u32[]{:S(2)}) copy-start(f32[1024]{0:T(1024)} %param.23) | copy-start | bytes 12292
  119.9 112.0 %copy-start.35 = (f32[1024]{0:T(1024)S(1)}, f32[1024]{0:T(1024)}, u32[]{:S(2)}) copy-start(f32[1024]{0:T(1024)} %param.24) | copy-start | bytes 12292
  283.2 12.8 %copy-start.33 = (bf16[1024,2048]{1,0:T(8,128)(2,1)S(1)}, bf16[1024,2048]{1,0:T(8,128)(2,1)}, u32[]{:S(2)}) copy-start(bf16[1024,2048]{1,0:T(8,128)(2,1)} %all-gather.6.cloned.1.call-done) | copy-start | bytes 12582916
  307.7 228.0 %reduce-scatter.16.cloned.1.call-start = ((), (), s32[]{:S(2)}) async-start(), calls=%async_computation.15 | async-start | bytes 557056 | tf_op jit(solution)/shard_map/reduce_scatter | solution.py:229
  459.3 115.3 %reduce-scatter.12.cloned.1.call-start = ((), (), s32[]{:S(2)}) async-start(), calls=%async_computation.13 | async-start | bytes 557056 | tf_op jit(solution)/shard_map/reduce_scatter | solution.py:218
  465.9 169.2 %reduce-scatter.14.cloned.1.call-start = ((), (), s32[]{:S(2)}) async-start(), calls=%async_computation.14 | async-start | bytes 1114112 | tf_op jit(solution)/shard_map/reduce_scatter | solution.py:221
  476.8 234.4 %reduce-scatter.18.cloned.1.call-start = ((), (), s32[]{:S(2)}) async-start(), calls=%async_computation.16 | async-start | bytes 4456448 | tf_op jit(solution)/shard_map/reduce_scatter | solution.py:224
  486.6 299.9 %reduce-scatter.20.cloned.1.call-start = ((), (), s32[]{:S(2)}) async-start(), calls=%async_computation.17 | async-start | bytes 4456448 | tf_op jit(solution)/shard_map/reduce_scatter | solution.py:232
  496.4 323.8 %reduce-scatter.10.cloned.1.call-start = ((), (), s32[]{:S(2)}) async-start(), calls=%async_computation.12 | async-start | bytes 3145728 | tf_op jit(solution)/shard_map/reduce_scatter | solution.py:193
  502.0 420.2 %reduce-scatter.8.cloned.1.call-start = ((), (), s32[]{:S(2)}) async-start(), calls=%async_computation.11 | async-start | bytes 12582912 | tf_op jit(solution)/shard_map/reduce_scatter | solution.py:190
  531.0 289.2 %copy-start.25 = (f32[1024]{0:T(1024)S(1)}, f32[1024]{0:T(1024)}, u32[]{:S(2)}) copy-start(f32[1024]{0:T(1024)} %param.21) | copy-start | bytes 12292
  535.6 290.7 %copy-start.23 = (bf16[16,64,1024]{2,1,0:T(8,128)(2,1)S(1)}, bf16[16,64,1024]{2,1,0:T(8,128)(2,1)}, u32[]{:S(2)}) copy-start(bf16[16,64,1024]{2,1,0:T(8,128)(2,1)} %get-tuple-element.44) | copy-start | bytes 6291460
  826.3 95.9 %copy-start.27 = (f32[1024]{0:T(1024)S(1)}, f32[1024]{0:T(1024)}, u32[]{:S(2)}) copy-start(f32[1024]{0:T(1024)} %param.19) | copy-start | bytes 12292
  922.2 7.6 copy-start.5
  (28 other events, 110.9 us)
Sparse Core Ops, SparseCore 0:
  10.8 41.0 all-gather.3
  117.2 61.6 all-reduce.3
  181.3 50.5 all-gather.5
  234.1 49.0 all-gather.7
  307.8 106.6 all-reduce.5
  459.4 55.7 reduce-scatter.15
  519.8 54.7 reduce-scatter.11
  578.8 56.3 reduce-scatter.13
  639.5 71.7 reduce-scatter.17
  714.9 71.4 reduce-scatter.19
  789.4 30.7 reduce-scatter.9
  822.9 99.2 reduce-scatter.7
